TPU v7x, 32 devices: a whole 2x2x4 slice. The times are simulated.
32 devices in a mesh: dp: 4 (over z), seq: 8 (over y, x, core).
Axes of the slice: x: 2, y: 2, z: 4, core: 2. Of those that a mesh axis runs over, the one named last changes fastest.
Arguments:
- inputs: bfloat16 [16, 2048, 896], P('dp', 'seq'), may hold values from -6 to 6
- cotangent: bfloat16 [16, 2048, 896], P('dp', 'seq'), may hold values from -6 to 6
- segments: int32 [16, 2048], P('dp', 'seq'), may hold values from 0 to 10, as said below
- positions: int32 [16, 2048], P('dp', 'seq'), may hold values from 0 to 3998, as said below
- attn_master: float32 [1838080], P('seq')
- attn_moment: float32 [1838080], P('seq'), may hold values from -0.3 to 0.3
- attn_second: float32 [1838080], P('seq'), may hold values from 0.001 to 0.1
- ffn_master: float32 [13074432], P('seq')
- ffn_moment: float32 [13074432], P('seq'), may hold values from -0.3 to 0.3
- ffn_second: float32 [13074432], P('seq'), may hold values from 0.001 to 0.1
Outputs:
- result: bfloat16 [16, 2048, 896], P('dp', 'seq')
- grad_input: float32 [16, 2048, 896], P('dp', 'seq')
- attn_change: float32 [1838080], P('seq')
- moment_attn: float32 [1838080], P('seq')
- second_attn: float32 [1838080], P('seq')
- grad_attn: float32 [1838080], P('seq')
- ffn_change: float32 [13074432], P('seq')
- moment_ffn: float32 [13074432], P('seq')
- second_ffn: float32 [13074432], P('seq')
- grad_ffn: float32 [13074432], P('seq')
Inputs may be any that keep to these rules, and one draw needn't show every extreme that they name: `segments`: in each sequence the document number starts at 0 and rises by one where a new document begins; every document has 200 to 2000 tokens, except the last of a sequence, which may be cut shorter. `positions`: A token's position is its index within its document plus an offset of 0 to 1999 drawn for each document.
All inputs are finite; a program needn't handle non-finite values.
Results may differ from a plain program's by a relative error of at most 0.025.
Values may be sent and summed in bfloat16 or wider, within the bound.
A program may use at most 640 MiB of HBM per device.

v0:
```python
import math

import jax
import jax.numpy as jnp
from jax import lax
from jax.sharding import PartitionSpec as P

D = 896
H = 14
KV = 2
HD = 64
FF = 4864
STEP = 8


norm_eps = 1e-06
rope_base = 1000000.0
first_decay = 0.9
second_decay = 0.95
learn_rate = 0.01
weight_decay = 0.1
adam_eps = 1e-08
masked_score = -1e30


def split_weights(attn_flat, ffn_flat):
    kv_width = KV * HD
    qkv_width = D + 2 * kv_width
    offset = 2 * D + qkv_width
    gain_one = attn_flat[0:D].astype(jnp.float32)
    gain_two = attn_flat[D : 2 * D].astype(jnp.float32)
    bias_qkv = attn_flat[2 * D : offset].astype(jnp.float32)
    w_qkv = attn_flat[offset : offset + D * qkv_width].reshape(D, qkv_width)
    w_out = attn_flat[offset + D * qkv_width : offset + D * qkv_width + D * D].reshape(D, D)
    w_gu = ffn_flat[: 2 * D * FF].reshape(D, 2 * FF)
    w_down = ffn_flat[2 * D * FF :].reshape(FF, D)
    return (gain_one, gain_two, bias_qkv, w_qkv, w_out, w_gu, w_down)


def rope_tables(pos_values):
    halfway = HD // 2
    frequency = jnp.exp(jnp.arange(halfway, dtype=jnp.float32) * (-2.0 * math.log(rope_base) / HD))
    angles = pos_values.astype(jnp.float32)[..., None] * frequency
    return (jnp.cos(angles), jnp.sin(angles))


def rotate(values, cosine, sine_table):
    halfway = values.shape[-1] // 2
    front_half = values[..., :halfway]
    back_half = values[..., halfway:]
    return jnp.concatenate(
        [
            front_half * cosine - back_half * sine_table,
            back_half * cosine + front_half * sine_table,
        ],
        axis=-1,
    )


def rotate_back(gradient, cosine, sine_table):
    halfway = gradient.shape[-1] // 2
    front_half = gradient[..., :halfway]
    back_half = gradient[..., halfway:]
    return jnp.concatenate(
        [
            front_half * cosine + back_half * sine_table,
            back_half * cosine - front_half * sine_table,
        ],
        axis=-1,
    )


def norm_back(values, inverse, gain, grad_norm):
    weighted = grad_norm * gain
    grad_gain = jnp.sum(grad_norm * values * inverse, axis=(0, 1))
    grad_in = inverse * weighted - values * inverse**3 * jnp.mean(
        values * weighted, axis=-1, keepdims=True
    )
    return (grad_in, grad_gain)


def adam_step(master, moment, second, gradient):
    moment_new = first_decay * moment + (1.0 - first_decay) * gradient
    second_new = second_decay * second + (1.0 - second_decay) * gradient * gradient
    corrected = moment_new / (1.0 - first_decay**STEP)
    spread_root = jnp.sqrt(second_new / (1.0 - second_decay**STEP))
    change = -learn_rate * (corrected / (spread_root + adam_eps) + weight_decay * master)
    return (change, moment_new, second_new)


def per_device(
    inputs,
    cotangent,
    segments,
    positions,
    attn_master,
    attn_moment,
    attn_second,
    ffn_master,
    ffn_moment,
    ffn_second,
):
    seq_count = inputs.shape[0]
    local_rows = inputs.shape[1]
    seq_parts = lax.axis_size("seq")
    seq_length = local_rows * seq_parts
    seq_rank = lax.axis_index("seq")
    token_scale = 1.0 / math.sqrt(seq_count * seq_length * lax.axis_size("dp"))
    kv_width = KV * HD
    groups = H // KV
    score_scale = HD ** (-0.5)
    attn_flat, ffn_flat = (
        lax.all_gather(attn_master.astype(jnp.bfloat16), "seq", axis=0, tiled=True),
        lax.all_gather(ffn_master.astype(jnp.bfloat16), "seq", axis=0, tiled=True),
    )
    gain_one, gain_two, bias_qkv, w_qkv, w_out, w_gu, w_down = split_weights(attn_flat, ffn_flat)
    x_wide = inputs.astype(jnp.float32)
    inv_one = lax.rsqrt(jnp.mean(x_wide * x_wide, axis=-1, keepdims=True) + norm_eps)
    normed_one = (x_wide * inv_one * gain_one).astype(jnp.bfloat16)
    qkv_proj = (
        jnp.einsum("scd,de->sce", normed_one, w_qkv, preferred_element_type=jnp.float32) + bias_qkv
    )
    cosine, sine_table = rope_tables(positions)
    cos_query = cosine[:, :, None, None, :]
    sin_query = sine_table[:, :, None, None, :]
    cos_key = cosine[:, :, None, :]
    sin_key = sine_table[:, :, None, :]
    queries = rotate(
        qkv_proj[..., :D].reshape(seq_count, local_rows, KV, groups, HD), cos_query, sin_query
    ).astype(jnp.bfloat16)
    key_rows = rotate(
        qkv_proj[..., D : D + kv_width].reshape(seq_count, local_rows, KV, HD), cos_key, sin_key
    )
    key_rows = key_rows.astype(jnp.bfloat16).reshape(seq_count, local_rows, kv_width)
    value_rows = qkv_proj[..., D + kv_width :].astype(jnp.bfloat16)
    key_all, value_all, seg_all = (
        lax.all_gather(key_rows, "seq", axis=1, tiled=True),
        lax.all_gather(value_rows, "seq", axis=1, tiled=True),
        lax.all_gather(segments.astype(jnp.bfloat16), "seq", axis=1, tiled=True),
    )
    key_span = min(512, seq_length)
    block_count = seq_length // key_span
    query_place = seq_rank * local_rows + jnp.arange(local_rows, dtype=jnp.int32)
    seg_query = segments.astype(jnp.float32)
    nothing = jnp.zeros((), jnp.float32)

    def block_parts(block_index):
        first_key = block_index * key_span
        key_block = key_all[:, first_key : first_key + key_span].reshape(
            seq_count, key_span, KV, HD
        )
        value_block = value_all[:, first_key : first_key + key_span].reshape(
            seq_count, key_span, KV, HD
        )
        key_place = first_key + jnp.arange(key_span, dtype=jnp.int32)
        seg_keys = seg_all[:, first_key : first_key + key_span].astype(jnp.float32)
        allowed = (seg_query[:, :, None] == seg_keys[:, None, :]) & (
            query_place[None, :, None] >= key_place[None, None, :]
        )
        return (key_block, value_block, allowed)

    def block_scores(key_block, allowed):
        raw_scores = (
            jnp.einsum("sckgd,sbkd->skgcb", queries, key_block, preferred_element_type=jnp.float32)
            * score_scale
        )
        return jnp.where(allowed[:, None, None, :, :], raw_scores, masked_score)

    row_peak = jnp.full((seq_count, KV, groups, local_rows), masked_score, jnp.float32)
    exp_total = jnp.zeros((seq_count, KV, groups, local_rows), jnp.float32)
    for block_index in range(block_count):
        key_block, value_block, allowed = block_parts(block_index)

        def first_pass(carried, key_block=key_block, allowed=allowed):
            peak_old, total_old = carried
            masked = block_scores(key_block, allowed)
            peak_new = jnp.maximum(peak_old, jnp.max(masked, axis=-1))
            total_new = total_old * jnp.exp(peak_old - peak_new) + jnp.sum(
                jnp.exp(masked - peak_new[..., None]), axis=-1
            )
            return ((peak_new, total_new), nothing)

        (row_peak, exp_total), unused = first_pass((row_peak, exp_total))
    log_total = row_peak + jnp.log(exp_total)
    mixed_heads = jnp.zeros((seq_count, local_rows, KV, groups, HD), jnp.float32)
    for block_index in range(block_count):
        key_block, value_block, allowed = block_parts(block_index)

        def second_pass(carried, key_block=key_block, value_block=value_block, allowed=allowed):
            masked = block_scores(key_block, allowed)
            soft_prob = jnp.exp(masked - log_total[..., None]).astype(jnp.bfloat16)
            added = jnp.einsum(
                "skgcb,sbkd->sckgd", soft_prob, value_block, preferred_element_type=jnp.float32
            )
            return (carried + added, nothing)

        mixed_heads, unused = second_pass(mixed_heads)
    mixed_low = mixed_heads.reshape(seq_count, local_rows, D).astype(jnp.bfloat16)
    branch = jnp.einsum("sci,io->sco", mixed_low, w_out, preferred_element_type=jnp.float32)
    residual = x_wide + branch
    inv_two = lax.rsqrt(jnp.mean(residual * residual, axis=-1, keepdims=True) + norm_eps)
    normed_two = (residual * inv_two * gain_two).astype(jnp.bfloat16)
    gate_up = jnp.einsum("scd,df->scf", normed_two, w_gu, preferred_element_type=jnp.float32)
    gate_part = gate_up[..., :FF]
    up_part = gate_up[..., FF:]
    sigmoid_gate = jax.nn.sigmoid(gate_part)
    silu_gate = gate_part * sigmoid_gate
    hidden = (silu_gate * up_part).astype(jnp.bfloat16)
    result = (
        residual + jnp.einsum("scf,fd->scd", hidden, w_down, preferred_element_type=jnp.float32)
    ).astype(jnp.bfloat16)
    grad_down = jnp.einsum("scf,scd->fd", hidden, cotangent, preferred_element_type=jnp.float32)
    grad_hidden = jnp.einsum("scd,fd->scf", cotangent, w_down, preferred_element_type=jnp.float32)
    grad_gate = grad_hidden * up_part * sigmoid_gate * (1.0 + gate_part * (1.0 - sigmoid_gate))
    grad_up = grad_hidden * silu_gate
    grad_gu = jnp.concatenate([grad_gate, grad_up], axis=-1).astype(jnp.bfloat16)
    grad_w_gu = jnp.einsum("scd,scf->df", normed_two, grad_gu, preferred_element_type=jnp.float32)
    grad_normed_two = jnp.einsum("scf,df->scd", grad_gu, w_gu, preferred_element_type=jnp.float32)
    grad_in_two, grad_gain_two = norm_back(residual, inv_two, gain_two, grad_normed_two)
    grad_residual = cotangent.astype(jnp.float32) + grad_in_two
    ffn_local = jnp.concatenate([grad_w_gu.reshape(-1), grad_down.reshape(-1)]) * token_scale
    grad_branch = grad_residual.astype(jnp.bfloat16)
    grad_w_out = jnp.einsum(
        "sci,sco->io", mixed_low, grad_branch, preferred_element_type=jnp.float32
    )
    grad_mixed = jnp.einsum("sco,io->sci", grad_branch, w_out, preferred_element_type=jnp.float32)
    grad_mixed = grad_mixed.astype(jnp.bfloat16).reshape(seq_count, local_rows, KV, groups, HD)
    row_delta = jnp.zeros((seq_count, KV, groups, local_rows), jnp.float32)
    for block_index in range(block_count):
        key_block, value_block, allowed = block_parts(block_index)

        def delta_pass(carried, key_block=key_block, value_block=value_block, allowed=allowed):
            masked = block_scores(key_block, allowed)
            soft_prob = jnp.exp(masked - log_total[..., None])
            grad_prob = jnp.einsum(
                "sckgd,sbkd->skgcb", grad_mixed, value_block, preferred_element_type=jnp.float32
            )
            return (carried + jnp.sum(soft_prob * grad_prob, axis=-1), nothing)

        row_delta, unused = delta_pass(row_delta)
    grad_queries = jnp.zeros((seq_count, local_rows, KV, groups, HD), jnp.float32)
    key_pieces = []
    value_pieces = []
    for block_index in range(block_count):
        key_block, value_block, allowed = block_parts(block_index)

        def grad_pass(carried, key_block=key_block, value_block=value_block, allowed=allowed):
            masked = block_scores(key_block, allowed)
            soft_prob = jnp.exp(masked - log_total[..., None])
            prob_low = soft_prob.astype(jnp.bfloat16)
            grad_prob = jnp.einsum(
                "sckgd,sbkd->skgcb", grad_mixed, value_block, preferred_element_type=jnp.float32
            )
            grad_score = (soft_prob * (grad_prob - row_delta[..., None])).astype(jnp.bfloat16)
            query_add = (
                jnp.einsum(
                    "skgcb,sbkd->sckgd", grad_score, key_block, preferred_element_type=jnp.float32
                )
                * score_scale
            )
            grad_key = (
                jnp.einsum(
                    "skgcb,sckgd->sbkd", grad_score, queries, preferred_element_type=jnp.float32
                )
                * score_scale
            )
            grad_value = jnp.einsum(
                "skgcb,sckgd->sbkd", prob_low, grad_mixed, preferred_element_type=jnp.float32
            )
            return (
                carried + query_add,
                (
                    grad_key.reshape(seq_count, key_span, kv_width),
                    grad_value.reshape(seq_count, key_span, kv_width),
                ),
            )

        grad_queries, block_grads = grad_pass(grad_queries)
        key_pieces.append(block_grads[0])
        value_pieces.append(block_grads[1])
    key_grad_all = jnp.concatenate(key_pieces, axis=1)
    value_grad_all = jnp.concatenate(value_pieces, axis=1)
    key_grad, value_grad = (
        lax.psum_scatter(
            key_grad_all.astype(jnp.bfloat16), "seq", scatter_dimension=1, tiled=True
        ).astype(jnp.float32),
        lax.psum_scatter(
            value_grad_all.astype(jnp.bfloat16), "seq", scatter_dimension=1, tiled=True
        ).astype(jnp.float32),
    )
    query_pre = rotate_back(grad_queries, cos_query, sin_query).reshape(seq_count, local_rows, D)
    key_pre = rotate_back(
        key_grad.reshape(seq_count, local_rows, KV, HD), cos_key, sin_key
    ).reshape(seq_count, local_rows, kv_width)
    grad_qkv = jnp.concatenate([query_pre, key_pre, value_grad], axis=-1).astype(jnp.bfloat16)
    grad_bias = jnp.sum(grad_qkv.astype(jnp.float32), axis=(0, 1))
    grad_w_qkv = jnp.einsum("scd,sce->de", normed_one, grad_qkv, preferred_element_type=jnp.float32)
    grad_normed_one = jnp.einsum("sce,de->scd", grad_qkv, w_qkv, preferred_element_type=jnp.float32)
    grad_in_one, grad_gain_one = norm_back(x_wide, inv_one, gain_one, grad_normed_one)
    grad_input = grad_residual + grad_in_one
    used_entries = 3 * D + 2 * kv_width + D * (2 * D + 2 * kv_width)
    padding = attn_master.shape[0] * seq_parts - used_entries
    attn_local = (
        jnp.concatenate(
            [
                grad_gain_one,
                grad_gain_two,
                grad_bias,
                grad_w_qkv.reshape(-1),
                grad_w_out.reshape(-1),
                jnp.zeros((padding,), jnp.float32),
            ]
        )
        * token_scale
    )
    attn_owned, ffn_owned = (
        lax.psum_scatter(
            attn_local.astype(jnp.bfloat16), "seq", scatter_dimension=0, tiled=True
        ).astype(jnp.float32),
        lax.psum_scatter(
            ffn_local.astype(jnp.bfloat16), "seq", scatter_dimension=0, tiled=True
        ).astype(jnp.float32),
    )
    grad_attn, grad_ffn = (
        lax.psum(attn_owned.astype(jnp.bfloat16), "dp").astype(jnp.float32),
        lax.psum(ffn_owned.astype(jnp.bfloat16), "dp").astype(jnp.float32),
    )
    attn_change, moment_attn, second_attn = adam_step(
        attn_master, attn_moment, attn_second, grad_attn
    )
    ffn_change, moment_ffn, second_ffn = adam_step(ffn_master, ffn_moment, ffn_second, grad_ffn)
    return (
        result,
        grad_input,
        attn_change,
        moment_attn,
        second_attn,
        grad_attn,
        ffn_change,
        moment_ffn,
        second_ffn,
        grad_ffn,
    )


def solution(mesh):
    in_specs = (
        P("dp", "seq", None),
        P("dp", "seq", None),
        P("dp", "seq"),
        P("dp", "seq"),
        P("seq"),
        P("seq"),
        P("seq"),
        P("seq"),
        P("seq"),
        P("seq"),
    )
    out_specs = (
        P("dp", "seq", None),
        P("dp", "seq", None),
        P("seq"),
        P("seq"),
        P("seq"),
        P("seq"),
        P("seq"),
        P("seq"),
        P("seq"),
        P("seq"),
    )
    return jax.shard_map(
        per_device, mesh=mesh, in_specs=in_specs, out_specs=out_specs, check_vma=False
    )
```

profile of v0, /device:TPU:0, one launch (start us, length us, event | category | flops | bytes accessed | tf_op | source)
XLA Modules:
  0.0 1687.3 jit_solution(13379455358743474625)
XLA Ops:
  17.3 50.1 %all-gather.12.cloned.1.call-done = bf16[8,1,229760]{2,1,0:T(2,128)(2,1)} async-done(((bf16[1,1,229760]{2,1,0:T(2,128)(2,1)}), bf16[8,1,229760]{2,1,0:T(2,128)(2,1)}) %all-gather.12.cloned.1.call-update) | async-done | bytes 3676176 | tf_op jit(solution)/shard_map/all_gather | solution.py:113
  67.4 79.1 %reduce = bf16[8,229760]{1,0:T(8,128)(2,1)} reduce(bf16[8,1,229760]{2,1,0:T(2,128)(2,1)} %all-gather.12.cloned.1.call-done, bf16[]{:T(256)} %constant.76), dimensions={1}, to_apply=%all-gather.reduce_sub_computation | reduce | bytes 7352322 | tf_op jit(solution)/shard_map/all_gather | solution.py:113
  146.5 9.3 reshape.455
  179.0 8.9 all_gather.17
  218.9 10.9 all-gather.8.cloned.1.call-done
  232.4 15.9 fusion.20
  248.4 11.8 fusion.21
  260.2 11.8 fusion.19
  272.0 15.8 fusion.18
  287.9 17.6 %exponential_reduce_fusion = f32[4,2,7,256]{3,2,1,0:T(8,128)S(1)} fusion(f32[4,2,512,256,7]{3,2,4,1,0:T(8,128)} %get-tuple-element.80, f32[4,2,7,256]{3,2,1,0:T(8,128)S(1)} %get-tuple-element.30, pred[4,256,512]{1,2,0:T(8,128)(4,1)S(1)} %get-tuple-element.72), kind=kLoop, calls=%fused_computation.30 | loop fusion | flops 29345792 | bytes 29999104 | tf_op jit(solution)/shard_map/reduce_sum | solution.py:178
  312.4 13.2 exponential_reduce_fusion.2
  325.6 13.2 exponential_reduce_fusion.3
  339.0 15.2 fusion.54
  354.2 15.3 fusion.60
  369.5 14.8 fusion.57
  384.3 17.9 %add_convert_fusion.1 = bf16[4,2,64,7,256]{4,2,3,1,0:T(8,128)(2,1)} fusion(f32[4,2,64,7,256]{4,2,3,1,0:T(8,128)} %fusion.54, f32[4,2,64,7,256]{4,2,3,1,0:T(8,128)} %fusion.60, f32[4,2,64,7,256]{4,2,3,1,0:T(8,128)} %fusion.57, bf16[4,512,2,64,1]{1,3,4,2,0:T(8,128)(2,1)S(1)} %bitcast.284, f32[4,2,512,256,7]{3,2,4,1,0:T(8,128)} %get-tuple-element.80, ...), kind=kOutput, calls=%fused_computation.81 | convolution fusion | flops 972554240 | bytes 43311104 | tf_op jit(solution)/shard_map/skgcb,sbkd->sckgd/dot_general | solution.py:192
  409.1 12.5 slice.207
  421.7 29.8 %reshape.466 = bf16[896,9728,1]{1,0,2:T(8,128)(2,1)} reshape(bf16[8716288]{0:T(1024)(128)(2,1)} %slice.207) | data formatting | bytes 34865152 | tf_op jit(solution)/shard_map/slice | solution.py:35
  460.1 16.4 reshape.467
  476.6 30.4 %fusion.50 = f32[4,256,9728]{2,1,0:T(8,128)} fusion(bf16[896,9728,1]{1,0,2:T(8,128)(2,1)} %reshape.466, f32[4,256,896]{2,1,0:T(8,128)} %get-tuple-element.88, f32[896]{0:T(1024)S(1)} %copy-done.60, f32[4,256]{1,0:T(4,128)S(1)} %get-tuple-element.68), kind=kOutput, calls=%fused_computation.125 | convolution fusion | flops 17853710336 | bytes 60956160 | tf_op jit(solution)/shard_map/scd,df->scf/dot_general | solution.py:203
  507.0 30.5 %multiply_convert_fusion.1 = (bf16[4,256,4864]{2,1,0:T(8,128)(2,1)}, bf16[4,256,4864]{2,1,0:T(8,128)(2,1)}, bf16[4,256,4864]{2,1,0:T(8,128)(2,1)}) fusion(f32[4,256,9728]{2,1,0:T(8,128)} %fusion.50, bf16[4,256,896]{2,1,0:T(8,128)(2,1)S(1)} %copy-done.48, bf16[4864,896,1]{1,0,2:T(8,128)(2,1)} %reshape.467), kind=kOutput, calls=%fused_computation.41 | convolution fusion | flops 9000189952 | bytes 80281600 | tf_op jit(solution)/shard_map/scd,fd->scf/dot_general | solution.py:213
  537.5 30.4 %multiply_reduce_fusion = (f32[896]{0:T(1024)}, f32[4,256]{1,0:T(4,128)S(1)}, f32[4,256,896]{2,1,0:T(8,128)}) fusion(f32[4,256,896]{2,1,0:T(8,128)} %get-tuple-element.88, f32[4,256]{1,0:T(4,128)S(1)} %get-tuple-element.68, f32[896]{0:T(1024)S(1)} %copy-done.60, bf16[896,9728,1]{1,0,2:T(8,128)(2,1)} %reshape.466, ...), kind=kOutput, calls=%fused_computation.74 | convolution fusion | flops 17896308736 | bytes 44710912 | tf_op jit(solution)/shard_map/scf,df->scd/dot_general | solution.py:218
  579.3 13.8 fusion.46
  593.1 13.6 fusion.45
  606.7 13.6 fusion.44
  620.4 13.9 fusion.43
  634.3 11.6 fusion.93
  645.9 11.6 fusion.94
  657.5 11.7 fusion.95
  669.2 27.2 %convolution_bitcast_fusion = f32[896,9728]{1,0:T(8,128)} fusion(bf16[4,256,4864]{2,1,0:T(8,128)(2,1)} %get-tuple-element.34, bf16[4,256,4864]{2,1,0:T(8,128)(2,1)} %get-tuple-element.33, f32[4,256,896]{2,1,0:T(8,128)S(1)} %copy-done.32, f32[896]{0:T(1024)S(1)} %copy-done.60, f32[4,256]{1,0:T(4,128)S(1)} %get-tuple-element.68), kind=kOutput, calls=%fused_computation.38 | convolution fusion | flops 17893556224 | bytes 58465792 | tf_op jit(solution)/shard_map/scd,scf->df/dot_general | solution.py:217
  704.6 75.6 %fusion.7 = (f32[4,2,7,256]{3,2,1,0:T(8,128)}, f32[4,2,7,256]{3,2,1,0:T(8,128)}, f32[4,2,7,256]{3,2,1,0:T(8,128)}, f32[4,2,7,256]{3,2,1,0:T(8,128)}, f32[4,2,512,256,7]{3,2,4,1,0:T(8,128)}) fusion(f32[4,2,512,256,7]{3,2,4,1,0:T(8,128)} %get-tuple-element.84, f32[4,2,7,256]{3,2,1,0:T(8,128)S(1)} %copy-done.51, pred[4,256,512]{1,2,0:T(8,128)(4,1)S(1)} %copy-done.10, ...), kind=kOutput, calls=%fused_computation.14 | convolution fusion | flops 1086267392 | bytes 239624192 | tf_op jit(solution)/shard_map/sckgd,sbkd->skgcb/dot_general | solution.py:235
  781.1 92.1 %fusion.12 = (bf16[4,2,7,256,512]{3,4,2,1,0:T(8,128)(2,1)}, bf16[4,2,7,256,512]{3,4,2,1,0:T(8,128)(2,1)}, bf16[4,2,7,256,512]{3,4,2,1,0:T(8,128)(2,1)}, bf16[4,2,7,256,512]{3,4,2,1,0:T(8,128)(2,1)}) fusion(f32[4,2,512,256,7]{3,2,4,1,0:T(8,128)} %fusion.93, f32[4,2,512,256,7]{3,2,4,1,0:T(8,128)} %get-tuple-element.86, f32[4,2,7,256]{3,2,1,0:T(8,128)S(1)} %add_add_fusion, ...), kind=kLoop, calls=%fused_computation.21 | loop fusion | flops 176160768 | bytes 295813120 | tf_op jit(solution)/shard_map/convert_element_type | solution.py:254
  873.2 9.7 fusion.42
  882.9 9.7 fusion.41
  892.6 9.7 fusion.40
  902.3 10.5 fusion.39
  915.5 17.5 %convolution_bitcast_fusion.1 = f32[4864,896]{1,0:T(8,128)} fusion(bf16[4,256,4864]{2,1,0:T(8,128)(2,1)} %get-tuple-element.35, bf16[4,256,896]{2,1,0:T(8,128)(2,1)} %param.11), kind=kOutput, calls=%fused_computation.50 | convolution fusion | flops 8925478912 | bytes 29229056 | tf_op jit(solution)/shard_map/scf,scd->fd/dot_general | solution.py:212
  933.0 18.6 %reshape.451 = f32[4358144]{0:T(1024)} reshape(f32[4864,896]{1,0:T(8,128)} %convolution_bitcast_fusion.1) | data formatting | bytes 34865152 | tf_op jit(solution)/shard_map/reshape | solution.py:221
  951.6 33.4 %reshape.450 = f32[8716288]{0:T(1024)} reshape(f32[896,9728]{1,0:T(8,128)} %convolution_bitcast_fusion) | data formatting | bytes 69730304 | tf_op jit(solution)/shard_map/reshape | solution.py:221
  986.5 9.7 fusion.98
  996.2 9.6 fusion.96
  1005.9 27.8 %fusion = bf16[13074432]{0:T(1024)(128)(2,1)} fusion(f32[4358144]{0:T(1024)} %reshape.451, f32[8716288]{0:T(1024)} %reshape.450), kind=kLoop, calls=%fused_computation.1 | loop fusion | flops 39223296 | bytes 78446592 | tf_op jit(solution)/shard_map/convert_element_type | solution.py:321
  1089.2 36.1 %dynamic-update-slice.3 = f32[1838080]{0:T(1024)} dynamic-update-slice(f32[1838080]{0:T(1024)} %constant_dynamic-update-slice_fusion.1, f32[1032192]{0:T(1024)} %reshape.448, s32[]{} %constant.81) | dynamic-update-slice | bytes 8257540
  1125.2 26.8 %dynamic-update-slice.4 = f32[1838080]{0:T(1024)} dynamic-update-slice(f32[1838080]{0:T(1024)} %dynamic-update-slice.3, f32[802816]{0:T(1024)S(1)} %reshape.449, s32[]{} %constant.82) | dynamic-update-slice | bytes 6422532
  1160.5 356.4 %all-reduce.7.cloned.1.call-done = (bf16[1838080]{0:T(1024)(128)(2,1)}, bf16[13074432]{0:T(1024)(128)(2,1)}) async-done(((bf16[1838080]{0:T(1024)(128)(2,1)}, bf16[13074432]{0:T(1024)(128)(2,1)}), (bf16[1838080]{0:T(1024)(128)(2,1)}, bf16[13074432]{0:T(1024)(128)(2,1)})) %all-reduce.7.cloned.1.call-update) | async-done | bytes 29825040
  1522.2 17.4 %add_convert_fusion = bf16[4,256,896]{2,1,0:T(8,128)(2,1)} fusion(f32[4,256,896]{2,1,0:T(8,128)} %get-tuple-element.88, bf16[4,256,4864]{2,1,0:T(8,128)(2,1)} %get-tuple-element.35, bf16[4864,896,1]{1,0,2:T(8,128)(2,1)} %reshape.467), kind=kOutput, calls=%fused_computation.78 | convolution fusion | flops 8927313920 | bytes 24182784 | tf_op jit(solution)/shard_map/scf,fd->scd/dot_general | solution.py:210
  1542.0 120.7 %all-reduce.9.cloned.1.call-done = (bf16[229760]{0:T(1024)(128)(2,1)}, bf16[1634304]{0:T(1024)(128)(2,1)}) async-done(((bf16[229760]{0:T(1024)(128)(2,1)}, bf16[1634304]{0:T(1024)(128)(2,1)}), (bf16[229760]{0:T(1024)(128)(2,1)}, bf16[1634304]{0:T(1024)(128)(2,1)})) %all-reduce.9.cloned.1.call-update) | async-done | bytes 3728144 | tf_op jit(solution)/shard_map/psum | solution.py:325
  1665.9 14.3 add_multiply_fusion
  (247 shorter events, 187.3 us)
Async XLA Ops:
  7.2 60.2 %all-gather.12.cloned.1.call-start = ((), (), s32[]{:S(2)}) async-start(), calls=%async_computation.7 | async-start | bytes 8271360 | tf_op jit(solution)/shard_map/all_gather | solution.py:113
  14.5 192.7 %all-gather.6.cloned.1.call-start = ((), (), s32[]{:S(2)}) async-start(), calls=%async_computation.2 | async-start | bytes 2359296 | tf_op jit(solution)/shard_map/all_gather | solution.py:138
  17.3 146.4 %copy-start.56 = (f32[4,256]{1,0:T(4,128)}, f32[4,256]{1,0:T(4,128)S(1)}, u32[]{:S(2)}) copy-start(f32[4,256]{1,0:T(4,128)S(1)} %get-tuple-element.66) | copy-start | bytes 12292
  171.7 58.2 %all-gather.8.cloned.1.call-start = ((), (), s32[]{:S(2)}) async-start(), calls=%async_computation.3 | async-start | bytes 2359296 | tf_op jit(solution)/shard_map/all_gather | solution.py:137
  172.3 32.1 %copy-start.34 = (f32[4,256,32]{1,2,0:T(8,128)}, f32[4,256,32]{1,2,0:T(8,128)S(1)}, u32[]{:S(2)}) copy-start(f32[4,256,32]{1,2,0:T(8,128)S(1)} %get-tuple-element.63) | copy-start | bytes 393220
  172.3 32.1 %copy-start.36 = (f32[4,256,32]{1,2,0:T(8,128)}, f32[4,256,32]{1,2,0:T(8,128)S(1)}, u32[]{:S(2)}) copy-start(f32[4,256,32]{1,2,0:T(8,128)S(1)} %get-tuple-element.64) | copy-start | bytes 393220
  174.6 234.5 %all-gather.10.cloned.1.call-start = ((), (), s32[]{:S(2)}) async-start(), calls=%async_computation.4 | async-start | bytes 29417472 | tf_op jit(solution)/shard_map/all_gather | solution.py:114
  178.9 883.4 %reduce-scatter.3.cloned.1.call-start = ((), (), s32[]{:S(2)}) async-start(), calls=%async_computation.5 | async-start | bytes 2359296 | tf_op jit(solution)/shard_map/reduce_scatter | solution.py:284
  191.0 69.2 %copy-start.8 = (pred[4,256,512]{1,2,0:T(8,128)(4,1)}, pred[4,256,512]{1,2,0:T(8,128)(4,1)S(1)}, u32[]{:S(2)}) copy-start(pred[4,256,512]{1,2,0:T(8,128)(4,1)S(1)} %get-tuple-element.70) | copy-start | bytes 1572868
  191.0 193.3 %copy-start.4 = (pred[4,256,512]{1,2,0:T(8,128)(4,1)}, pred[4,256,512]{1,2,0:T(8,128)(4,1)S(1)}, u32[]{:S(2)}) copy-start(pred[4,256,512]{1,2,0:T(8,128)(4,1)S(1)} %get-tuple-element.72) | copy-start | bytes 1572868
  207.1 64.8 %copy-start = (bf16[4,256,2,7,32]{1,4,3,2,0:T(8,128)(2,1)}, bf16[4,256,2,7,32]{1,4,3,2,0:T(8,128)(2,1)S(1)}, u32[]{:S(2)}) copy-start(bf16[4,256,2,7,32]{1,4,3,2,0:T(8,128)(2,1)S(1)} %get-tuple-element.38) | copy-start | bytes 2752516
  207.2 64.8 %copy-start.2 = (bf16[4,256,2,7,32]{1,4,3,2,0:T(8,128)(2,1)}, bf16[4,256,2,7,32]{1,4,3,2,0:T(8,128)(2,1)S(1)}, u32[]{:S(2)}) copy-start(bf16[4,256,2,7,32]{1,4,3,2,0:T(8,128)(2,1)S(1)} %get-tuple-element.39) | copy-start | bytes 2752516
  232.4 15.9 copy-start.27
  232.4 15.9 copy-start.22
  232.4 27.8 %copy-start.24 = (bf16[4,512,128]{1,2,0:T(8,128)(2,1)}, bf16[4,512,128]{1,2,0:T(8,128)(2,1)S(1)}, u32[]{:S(2)}) copy-start(bf16[4,512,128]{1,2,0:T(8,128)(2,1)S(1)} %get-tuple-element.49) | copy-start | bytes 1572868
  272.0 33.5 %slice-start = ((s8[29360128]{0:T(1024)(128)(4,1)}), s8[4194304]{0:T(1024)(128)(4,1)S(1)}, s32[]{:S(2)}) async-start(s8[29360128]{0:T(1024)(128)(4,1)} %bitcast.272), calls=%async_computation.10 | async-start | bytes 8388608
  272.0 33.5 %slice-start.1 = ((s8[29360128]{0:T(1024)(128)(4,1)}), s8[4194304]{0:T(1024)(128)(4,1)S(1)}, s32[]{:S(2)}) async-start(s8[29360128]{0:T(1024)(128)(4,1)} %bitcast.272), calls=%async_computation.11 | async-start | bytes 8388608
  272.0 33.5 %slice-start.2 = ((s8[29360128]{0:T(1024)(128)(4,1)}), s8[4194304]{0:T(1024)(128)(4,1)S(1)}, s32[]{:S(2)}) async-start(s8[29360128]{0:T(1024)(128)(4,1)} %bitcast.272), calls=%async_computation.12 | async-start | bytes 8388608
  272.0 33.5 %slice-start.3 = ((s8[29360128]{0:T(1024)(128)(4,1)}), s8[4194304]{0:T(1024)(128)(4,1)S(1)}, s32[]{:S(2)}) async-start(s8[29360128]{0:T(1024)(128)(4,1)} %bitcast.272), calls=%async_computation.13 | async-start | bytes 8388608
  287.8 17.7 %slice-start.4 = ((s8[29360128]{0:T(1024)(128)(4,1)}), s8[4194304]{0:T(1024)(128)(4,1)S(1)}, s32[]{:S(2)}) async-start(s8[29360128]{0:T(1024)(128)(4,1)} %bitcast.272), calls=%async_computation.14 | async-start | bytes 8388608
  287.8 17.7 %slice-start.5 = ((s8[29360128]{0:T(1024)(128)(4,1)}), s8[4194304]{0:T(1024)(128)(4,1)S(1)}, s32[]{:S(2)}) async-start(s8[29360128]{0:T(1024)(128)(4,1)} %bitcast.272), calls=%async_computation.15 | async-start | bytes 8388608
  287.9 17.7 %slice-start.6 = ((s8[29360128]{0:T(1024)(128)(4,1)}), s8[4194304]{0:T(1024)(128)(4,1)S(1)}, s32[]{:S(2)}) async-start(s8[29360128]{0:T(1024)(128)(4,1)} %bitcast.272), calls=%async_computation.16 | async-start | bytes 8388608
  287.9 17.7 %copy-start.11 = (pred[4,256,512]{1,2,0:T(8,128)(4,1)S(1)}, pred[4,256,512]{1,2,0:T(8,128)(4,1)}, u32[]{:S(2)}) copy-start(pred[4,256,512]{1,2,0:T(8,128)(4,1)} %get-tuple-element.71) | copy-start | bytes 1572868
  338.9 45.4 %copy-start.50 = (f32[4,2,7,256]{3,2,1,0:T(8,128)}, f32[4,2,7,256]{3,2,1,0:T(8,128)S(1)}, u32[]{:S(2)}) copy-start(f32[4,2,7,256]{3,2,1,0:T(8,128)S(1)} %log_add_fusion) | copy-start | bytes 172036
  354.2 15.3 copy-start.39
  384.3 17.9 %copy-start.17 = (bf16[4,256,896]{2,1,0:T(8,128)(2,1)S(1)}, bf16[4,256,896]{2,1,0:T(8,128)(2,1)}, u32[]{:S(2)}) copy-start(bf16[4,256,896]{2,1,0:T(8,128)(2,1)} %param.10) | copy-start | bytes 5505028
  460.1 16.4 copy-start.60
  476.5 30.4 %copy-start.48 = (bf16[4,256,896]{2,1,0:T(8,128)(2,1)S(1)}, bf16[4,256,896]{2,1,0:T(8,128)(2,1)}, u32[]{:S(2)}) copy-start(bf16[4,256,896]{2,1,0:T(8,128)(2,1)} %param.11) | copy-start | bytes 5505028
  537.5 30.4 %copy-start.31 = (f32[4,256,896]{2,1,0:T(8,128)S(1)}, f32[4,256,896]{2,1,0:T(8,128)}, u32[]{:S(2)}) copy-start(f32[4,256,896]{2,1,0:T(8,128)} %get-tuple-element.88) | copy-start | bytes 11010052
  537.5 30.4 %copy-start.61 = (f32[4,256]{1,0:T(4,128)S(1)}, f32[4,256]{1,0:T(4,128)}, u32[]{:S(2)}) copy-start(f32[4,256]{1,0:T(4,128)} %get-tuple-element.67) | copy-start | bytes 12292
  781.1 92.1 %copy-start.1 = (bf16[4,256,2,7,32]{1,4,3,2,0:T(8,128)(2,1)S(1)}, bf16[4,256,2,7,32]{1,4,3,2,0:T(8,128)(2,1)}, u32[]{:S(2)}) copy-start(bf16[4,256,2,7,32]{1,4,3,2,0:T(8,128)(2,1)} %copy-done) | copy-start | bytes 2752516
  781.1 92.1 %copy-start.3 = (bf16[4,256,2,7,32]{1,4,3,2,0:T(8,128)(2,1)S(1)}, bf16[4,256,2,7,32]{1,4,3,2,0:T(8,128)(2,1)}, u32[]{:S(2)}) copy-start(bf16[4,256,2,7,32]{1,4,3,2,0:T(8,128)(2,1)} %copy-done.2) | copy-start | bytes 2752516
  915.5 149.8 %reduce-scatter.5.cloned.1.call-start = ((), (), s32[]{:S(2)}) async-start(), calls=%async_computation.6 | async-start | bytes 2359296 | tf_op jit(solution)/shard_map/reduce_scatter | solution.py:287
  951.6 33.4 %copy-start.44 = (bf16[4,512,128]{2,1,0:T(8,128)(2,1)S(1)}, bf16[4,512,128]{2,1,0:T(8,128)(2,1)}, u32[]{:S(2)}) copy-start(bf16[4,512,128]{2,1,0:T(8,128)(2,1)} %copy.127) | copy-start | bytes 1572868
  951.6 33.4 %copy-start.45 = (bf16[4,512,128]{2,1,0:T(8,128)(2,1)S(1)}, bf16[4,512,128]{2,1,0:T(8,128)(2,1)}, u32[]{:S(2)}) copy-start(bf16[4,512,128]{2,1,0:T(8,128)(2,1)} %copy.126) | copy-start | bytes 1572868
  951.6 33.4 %copy-start.46 = (bf16[4,512,128]{2,1,0:T(8,128)(2,1)S(1)}, bf16[4,512,128]{2,1,0:T(8,128)(2,1)}, u32[]{:S(2)}) copy-start(bf16[4,512,128]{2,1,0:T(8,128)(2,1)} %copy.125) | copy-start | bytes 1572868
  951.6 33.4 %copy-start.47 = (bf16[4,512,128]{2,1,0:T(8,128)(2,1)S(1)}, bf16[4,512,128]{2,1,0:T(8,128)(2,1)}, u32[]{:S(2)}) copy-start(bf16[4,512,128]{2,1,0:T(8,128)(2,1)} %copy.124) | copy-start | bytes 1572868
  951.6 34.9 %copy-start.28 = (bf16[4,512,128]{1,2,0:T(8,128)(2,1)S(1)}, bf16[4,512,128]{1,2,0:T(8,128)(2,1)}, u32[]{:S(2)}) copy-start(bf16[4,512,128]{1,2,0:T(8,128)(2,1)} %copy-done.27) | copy-start | bytes 1572868
  1005.9 27.9 %copy-start.25 = (bf16[4,512,128]{1,2,0:T(8,128)(2,1)S(1)}, bf16[4,512,128]{1,2,0:T(8,128)(2,1)}, u32[]{:S(2)}) copy-start(bf16[4,512,128]{1,2,0:T(8,128)(2,1)} %copy-done.24) | copy-start | bytes 1572868
  1005.9 511.0 %all-reduce.7.cloned.1.call-start = ((), (), s32[]{:S(2)}) async-start(), calls=%async_computation.8 | async-start | bytes 59650048
  1158.0 504.7 %all-reduce.9.cloned.1.call-start = ((), (), s32[]{:S(2)}) async-start(), calls=%async_computation.9 | async-start | bytes 7458816 | tf_op jit(solution)/shard_map/psum | solution.py:325
  1522.2 17.4 %copy-start.16 = (f32[4,256,896]{2,1,0:T(8,128)S(1)}, f32[4,256,896]{2,1,0:T(8,128)}, u32[]{:S(2)}) copy-start(f32[4,256,896]{2,1,0:T(8,128)} %copy-done.15) | copy-start | bytes 11010052
  1522.2 17.4 %copy-start.18 = (bf16[4,256,896]{2,1,0:T(8,128)(2,1)S(1)}, bf16[4,256,896]{2,1,0:T(8,128)(2,1)}, u32[]{:S(2)}) copy-start(bf16[4,256,896]{2,1,0:T(8,128)(2,1)} %param.10) | copy-start | bytes 5505028
  1522.2 17.4 %copy-start.33 = (f32[4,256,896]{2,1,0:T(8,128)S(1)}, f32[4,256,896]{2,1,0:T(8,128)}, u32[]{:S(2)}) copy-start(f32[4,256,896]{2,1,0:T(8,128)} %get-tuple-element.91) | copy-start | bytes 11010052
  1522.2 17.4 %copy-start.55 = (f32[4,256]{1,0:T(4,128)S(1)}, f32[4,256]{1,0:T(4,128)}, u32[]{:S(2)}) copy-start(f32[4,256]{1,0:T(4,128)} %get-tuple-element.65) | copy-start | bytes 12292
  1539.6 123.1 %copy-start.30 = (f32[229760]{0:T(1024)S(1)}, f32[229760]{0:T(1024)}, u32[]{:S(2)}) copy-start(f32[229760]{0:T(1024)} %param.14) | copy-start | bytes 2757124
  1539.6 123.1 %copy-start.52 = (f32[229760]{0:T(1024)S(1)}, f32[229760]{0:T(1024)}, u32[]{:S(2)}) copy-start(f32[229760]{0:T(1024)} %param.15) | copy-start | bytes 2757124
  1539.6 123.1 %copy-start.53 = (f32[229760]{0:T(1024)S(1)}, f32[229760]{0:T(1024)}, u32[]{:S(2)}) copy-start(f32[229760]{0:T(1024)} %param.16) | copy-start | bytes 2757124
  (33 other events, 291.6 us)
Sparse Core Ops, SparseCore 0:
  14.6 52.6 all-gather.11
  171.8 27.9 all-gather.5
  201.7 28.1 all-gather.7
  232.2 129.4 all-gather.9
  915.6 41.1 reduce-scatter.2
  1006.0 41.2 reduce-scatter.4
  1158.1 358.7 all-reduce.6
  1522.3 140.3 all-reduce.8
where the time goes:
time: 1700 us; the launch traced here: 1690 us
  matrix products  548 us (32%)
  waiting for transfers between devices  538 us (32%)
  other arithmetic  304 us (18%)
  local copies, waits for them, and re-layouts  271 us (16%)
    unnamed x9, waiting for transfers between devices  356 us
    psum x1, waiting for transfers between devices, per_device(): lax.psum(attn_owned.astype(jnp.bfloat16), 'dp').astype(jnp.float32)  121 us
    dot_general x3, matrix products, delta_pass(): jnp.einsum('sckgd,sbkd->skgcb', grad_mixed, value_block, preferred_elemen...  98.9 us
    unnamed x156, local copies, waits for them, and re-layouts  92.9 us
    convert_element_type x1, other arithmetic, grad_pass(): (soft_prob * (grad_prob - row_delta[..., None])).astype(jnp.bfloat16)  92.1 us
    all_gather x1, other arithmetic, per_device(): lax.all_gather(attn_master.astype(jnp.bfloat16), 'seq', axis=0, tiled=True)  79.1 us
    dot_general x4, matrix products, second_pass(): jnp.einsum('skgcb,sbkd->sckgd', soft_prob, value_block, preferred_element...  63.2 us
    dot_general x4, matrix products, block_scores(): jnp.einsum('sckgd,sbkd->skgcb', queries, key_block, preferred_element_typ...  55.3 us
  transfers between devices with their start and end apart: 8, of which 4 were waited for; matrix products, arithmetic and copies ran while one was open for 23% of the time, Pallas kernels for 0%

commit v1 on v0

v1 whole, which is shorter than its diff:
```python
import functools
import math

import jax
import jax.numpy as jnp
from jax import lax
from jax.experimental import pallas as pl
from jax.experimental.pallas import tpu as pltpu
from jax.sharding import PartitionSpec as P

D = 896
H = 14
KV = 2
GROUP = H // KV
HD = 64
FF = 4864
STEP = 8
QKV = D + 2 * KV * HD
F32 = jnp.float32
BF = jnp.bfloat16

norm_eps = 1e-06
rope_base = 1000000.0
first_decay = 0.9
second_decay = 0.95
learn_rate = 0.01
weight_decay = 0.1
adam_eps = 1e-08
masked_score = -1e30
MIB = 1 << 20

PIECE = 4256
PIECE_TILES = 532
GU_PIECES = 16
COLS = 2 * FF // 128
STEPS = FF // 256
GAIN_ROWS = (2 * D + QKV) // 128
OUT_ROW = GAIN_ROWS + D * QKV // 128
USED_ROWS = OUT_ROW + D * D // 128


def nn(a, b):
    return lax.dot_general(a, b, (((1,), (0,)), ((), ())), preferred_element_type=F32)


def nt(a, b):
    return lax.dot_general(a, b, (((1,), (1,)), ((), ())), preferred_element_type=F32)


def params(mib):
    return pltpu.CompilerParams(vmem_limit_bytes=mib * MIB)


def adam_step(master, moment, second, gradient):
    moment_new = first_decay * moment + (1.0 - first_decay) * gradient
    second_new = second_decay * second + (1.0 - second_decay) * gradient * gradient
    corrected = moment_new / (1.0 - first_decay**STEP)
    spread_root = jnp.sqrt(second_new / (1.0 - second_decay**STEP))
    change = -learn_rate * (corrected / (spread_root + adam_eps) + weight_decay * master)
    return (change, moment_new, second_new)


def pack_kernel(kind_ref, x_ref, o_ref):
    kind = kind_ref[pl.program_id(0)]

    @pl.when(kind == 0)
    def _():
        def body(c, _):
            for r in range(7):
                o_ref[c * 7 + r] = x_ref[pl.ds(r * 608 + c, 8, stride=COLS), :].astype(BF)
            return 0

        lax.fori_loop(0, COLS, body, 0, unroll=4)

    @pl.when(kind == 1)
    def _():
        def body(r, _):
            for c in range(7):
                o_ref[r * 7 + c] = x_ref[pl.ds(r * 56 + c, 8, stride=7), :].astype(BF)
            return 0

        lax.fori_loop(0, 76, body, 0, unroll=4)


def pack(kinds, flat):
    count = flat.shape[0] // PIECE
    return pl.pallas_call(
        pack_kernel,
        out_shape=jax.ShapeDtypeStruct((count * PIECE_TILES, 8, 128), BF),
        grid_spec=pltpu.PrefetchScalarGridSpec(
            num_scalar_prefetch=1,
            grid=(count,),
            in_specs=[pl.BlockSpec((PIECE, 128), lambda i, k: (i, 0))],
            out_specs=pl.BlockSpec((PIECE_TILES, 8, 128), lambda i, k: (i, 0, 0)),
        ),
        compiler_params=params(32),
        name="pack_ffn",
    )(kinds, flat)


def adam_kernel(kind_ref, g_ref, w_ref, m_ref, v_ref, ch_ref, mo_ref, se_ref, gr_ref):
    kind = kind_ref[pl.program_id(0)]

    @pl.when(kind == 0)
    def _():
        def body(c, _):
            for r in range(7):
                gr_ref[pl.ds(r * 608 + c, 8, stride=COLS), :] = g_ref[c * 7 + r].astype(F32)
            return 0

        lax.fori_loop(0, COLS, body, 0, unroll=4)

    @pl.when(kind == 1)
    def _():
        def body(r, _):
            for c in range(7):
                gr_ref[pl.ds(r * 56 + c, 8, stride=7), :] = g_ref[r * 7 + c].astype(F32)
            return 0

        lax.fori_loop(0, 76, body, 0, unroll=4)

    def update(i, _):
        rows = pl.ds(pl.multiple_of(i * 56, 8), 56)
        change, moment, second = adam_step(
            w_ref[rows, :], m_ref[rows, :], v_ref[rows, :], gr_ref[rows, :]
        )
        ch_ref[rows, :] = change
        mo_ref[rows, :] = moment
        se_ref[rows, :] = second
        return 0

    lax.fori_loop(0, PIECE // 56, update, 0)


def adam_tiles(kinds, tiles, master, moment, second):
    count = master.shape[0] // PIECE
    flat = pl.BlockSpec((PIECE, 128), lambda i, k: (i, 0))
    return pl.pallas_call(
        adam_kernel,
        out_shape=(jax.ShapeDtypeStruct(master.shape, F32),) * 4,
        grid_spec=pltpu.PrefetchScalarGridSpec(
            num_scalar_prefetch=1,
            grid=(count,),
            in_specs=[pl.BlockSpec((PIECE_TILES, 8, 128), lambda i, k: (i, 0, 0)), flat, flat, flat],
            out_specs=(flat,) * 4,
        ),
        compiler_params=params(48),
        name="adam_ffn",
    )(kinds, tiles, master, moment, second)


def tiles_of_flat(flat):
    cut = 2 * D * FF
    gu = flat[:cut].reshape(GU_PIECES, 7, 8, COLS, 128).transpose(0, 3, 1, 2, 4)
    down = flat[cut:].reshape(FF // 8, 8, 7, 128).transpose(0, 2, 1, 3)
    return jnp.concatenate([gu.reshape(-1, 8, 128), down.reshape(-1, 8, 128)])


def flat_of_tiles(tiles):
    cut = GU_PIECES * PIECE_TILES
    gu = tiles[:cut].reshape(GU_PIECES, COLS, 7, 8, 128).transpose(0, 2, 3, 1, 4)
    down = tiles[cut:].reshape(FF // 8, 7, 8, 128).transpose(0, 2, 1, 3)
    return jnp.concatenate([gu.reshape(-1), down.reshape(-1)])


def qkv_kernel(
    x_ref, flat_ref, cos_ref, sin_ref,
    qt_ref, kv_ref, nt_ref, wqkv_ref, wout_ref, gains_ref,
    wide, bias_s,
):
    tokens = x_ref.shape[0]
    span = kv_ref.shape[1]
    rows = flat_ref.shape[0]
    chunk = rows // 4
    chunk -= chunk % 16
    for i in range(4):
        lo, hi = i * chunk, (i + 1) * chunk if i < 3 else rows
        wide[lo:hi, :] = flat_ref[lo:hi, :].astype(F32)
    for c in range(7):
        lanes = slice(c * 128, (c + 1) * 128)
        gains_ref[0:1, lanes] = wide[c : c + 1, :]
        gains_ref[1:2, lanes] = wide[7 + c : 8 + c, :]
    for c in range(9):
        bias_s[0:1, c * 128 : (c + 1) * 128] = wide[14 + c : 15 + c, :]

    def unpack(r, _):
        out_rows = pl.ds(pl.multiple_of(r * 16, 16), 16)
        for c in range(9):
            wqkv_ref[out_rows, c * 128 : (c + 1) * 128] = wide[
                pl.ds(GAIN_ROWS + r * 144 + c, 16, stride=9), :
            ].astype(BF)
        for c in range(7):
            wout_ref[out_rows, c * 128 : (c + 1) * 128] = wide[
                pl.ds(OUT_ROW + r * 112 + c, 16, stride=7), :
            ].astype(BF)
        return 0

    lax.fori_loop(0, D // 16, unpack, 0, unroll=2)
    gain = gains_ref[0:1, :]
    for i in range(tokens // span):
        sl = slice(i * span, (i + 1) * span)
        x = x_ref[sl, :].astype(F32)
        inv = lax.rsqrt(jnp.mean(x * x, axis=1, keepdims=True) + norm_eps)
        normed = (x * inv * gain).astype(BF)
        nt_ref[:, sl] = normed.T
        proj = nn(normed, wqkv_ref[...]) + bias_s[...]
        cos, sin = cos_ref[:, sl], sin_ref[:, sl]
        turned = proj[:, : D + KV * HD].T
        for h in range(H + KV):
            a = turned[h * HD : h * HD + HD // 2, :]
            b = turned[h * HD + HD // 2 : (h + 1) * HD, :]
            front, back = a * cos - b * sin, b * cos + a * sin
            if h < H:
                qt_ref[h * HD : h * HD + HD // 2, sl] = (front.astype(BF) * 0.125).astype(BF)
                qt_ref[h * HD + HD // 2 : (h + 1) * HD, sl] = (back.astype(BF) * 0.125).astype(BF)
            else:
                k = h - H
                both = jnp.concatenate([front, back], axis=0).astype(BF)
                kv_ref[i, :, k * HD : (k + 1) * HD] = both.T
        kv_ref[i, :, KV * HD :] = proj[:, D + KV * HD :].astype(BF)


def qkv_forward(x, flat, cos, sin, count):
    tokens = x.shape[0]
    return pl.pallas_call(
        qkv_kernel,
        out_shape=(
            jax.ShapeDtypeStruct((D, tokens), BF),
            jax.ShapeDtypeStruct((count, tokens // count, 2 * KV * HD), BF),
            jax.ShapeDtypeStruct((D, tokens), BF),
            jax.ShapeDtypeStruct((D, QKV), BF),
            jax.ShapeDtypeStruct((D, D), BF),
            jax.ShapeDtypeStruct((2, D), F32),
        ),
        scratch_shapes=[pltpu.VMEM(flat.shape, F32), pltpu.VMEM((1, QKV), F32)],
        compiler_params=params(56),
        name="qkv_forward",
    )(x, flat, cos, sin)


def tail_kernel(
    scale, dq_ref, dkv_ref, x_ref, nt_ref, wqkv_ref, gains_ref, cos_ref, sin_ref, gres_ref, dwout_ref, ggain_ref,
    gin_ref, flat_ref, wide, gt_s, g_s,
):
    tokens = x_ref.shape[0]
    span = dkv_ref.shape[1]
    gt_s[0:D, :] = dq_ref[...]
    for i in range(tokens // span):
        sl = slice(i * span, (i + 1) * span)
        cos, sin = cos_ref[:, sl], sin_ref[:, sl]
        both = dkv_ref[i].T
        for k in range(KV):
            a = both[k * HD : k * HD + HD // 2, :].astype(F32)
            b = both[k * HD + HD // 2 : (k + 1) * HD, :].astype(F32)
            base = D + k * HD
            gt_s[base : base + HD // 2, sl] = (a * cos + b * sin).astype(BF)
            gt_s[base + HD // 2 : base + HD, sl] = (b * cos - a * sin).astype(BF)
        gt_s[D + KV * HD :, sl] = both[KV * HD :, :]
    gain = gains_ref[0:1, :]
    grad_gain = jnp.zeros((1, D), F32)
    grad_bias = jnp.zeros((1, QKV), F32)
    for i in range(tokens // span):
        sl = slice(i * span, (i + 1) * span)
        g = gt_s[:, sl].T
        g_s[sl, :] = g
        grad_bias += jnp.sum(g.astype(F32), axis=0, keepdims=True)
        gn = nt(g, wqkv_ref[...])
        x = x_ref[sl, :].astype(F32)
        inv = lax.rsqrt(jnp.mean(x * x, axis=1, keepdims=True) + norm_eps)
        grad_gain += jnp.sum(gn * (x * inv), axis=0, keepdims=True)
        weighted = gn * gain
        mean = jnp.mean(x * weighted, axis=1, keepdims=True)
        gin_ref[sl, :] = gres_ref[sl, :] + inv * weighted - x * (inv * inv * inv * mean)
    grad_gain *= scale
    grad_bias *= scale
    for c in range(7):
        lanes = slice(c * 128, (c + 1) * 128)
        wide[c : c + 1, :] = grad_gain[:, lanes]
        wide[7 + c : 8 + c, :] = ggain_ref[:, lanes]
    for c in range(9):
        wide[14 + c : 15 + c, :] = grad_bias[:, c * 128 : (c + 1) * 128]
    for q in range(0, D, 128):
        dw = nn(nt_ref[q : q + 128, :], g_s[...]) * scale
        for r in range(8):
            row = q + r * 16
            for c in range(9):
                wide[pl.ds(GAIN_ROWS + row * 9 + c, 16, stride=9), :] = dw[
                    r * 16 : (r + 1) * 16, c * 128 : (c + 1) * 128
                ]

    def pack_out(r, _):
        rows = pl.ds(pl.multiple_of(r * 16, 16), 16)
        for c in range(7):
            wide[pl.ds(OUT_ROW + r * 112 + c, 16, stride=7), :] = dwout_ref[
                rows, c * 128 : (c + 1) * 128
            ].astype(F32)
        return 0

    lax.fori_loop(0, D // 16, pack_out, 0, unroll=2)
    rows = flat_ref.shape[0]
    wide[USED_ROWS:rows, :] = jnp.zeros((rows - USED_ROWS, 128), F32)
    chunk = rows // 4
    chunk -= chunk % 16
    for i in range(4):
        lo, hi = i * chunk, (i + 1) * chunk if i < 3 else rows
        flat_ref[lo:hi, :] = wide[lo:hi, :].astype(BF)


def tail_backward(scale, rows, dq, dkv, x, normed_t, wqkv, gains, cos, sin, gres, dwout, ggain):
    tokens = x.shape[0]
    return pl.pallas_call(
        functools.partial(tail_kernel, scale),
        out_shape=(
            jax.ShapeDtypeStruct((tokens, D), F32),
            jax.ShapeDtypeStruct((rows, 128), BF),
        ),
        scratch_shapes=[
            pltpu.VMEM((rows, 128), F32),
            pltpu.VMEM((QKV, tokens), BF),
            pltpu.VMEM((tokens, QKV), BF),
        ],
        compiler_params=params(58),
        name="tail_backward",
    )(dq, dkv, x, normed_t, wqkv, gains, cos, sin, gres, dwout, ggain)


def bias_of(kb,st_ref,L,rank):
    rows=lax.broadcasted_iota(jnp.int32,(L,L),0)+kb*L
    qp=lax.broadcasted_iota(jnp.int32,(L,L),1)+rank*L
    return jnp.where((rows>=st_ref[0])&(rows<=qp),0.0,masked_score).astype(F32)
def fwd_kernel(lo_ref, qt_ref, kv_ref, st_ref, mix_ref, mixt_ref, lse_ref, m_s, l_s, o_s, bias_s):
    s=pl.program_id(0); L=qt_ref.shape[1]
    lo=lo_ref[s]; rank=lo_ref[4]
    m_s[...]=jnp.full_like(m_s, masked_score); l_s[...]=jnp.zeros_like(l_s); o_s[...]=jnp.zeros_like(o_s)
    def body(kb,_):
        bias_s[...]=bias_of(kb,st_ref,L,rank)
        kvb=kv_ref[kb,0]
        vt=kvb[:,128:].T
        for g in range(2):
            k=kvb[:,g*64:(g+1)*64]
            v=vt[g*64:(g+1)*64]
            for h in range(g*GROUP,(g+1)*GROUP):
                sl=slice(h*64,(h+1)*64)
                sc=nn(k,qt_ref[sl,:])+bias_s[...]
                mo=m_s[h:h+1,:]
                mn=jnp.maximum(mo,jnp.max(sc,axis=0,keepdims=True))
                p=jnp.exp(sc-mn)
                al=jnp.exp(mo-mn)
                m_s[h:h+1,:]=mn
                l_s[h:h+1,:]=l_s[h:h+1,:]*al+jnp.sum(p,axis=0,keepdims=True)
                o_s[sl,:]=o_s[sl,:]*al+nn(v,p.astype(BF))
        return 0
    lax.fori_loop(lo,rank+1,body,0)
    lse_ref[...]=(m_s[...]+jnp.log(l_s[...]))[None]
    for h in range(H):
        sl=slice(h*64,(h+1)*64)
        mixt_ref[sl,:]=(o_s[sl,:]*(1.0/l_s[h:h+1,:])).astype(BF)
    mix_ref[...]=mixt_ref[...].T
def attn_fwd(lo,qt,kv,starts):
    n=kv.shape[0]; nb=kv.shape[1]; L=kv.shape[2]; T=qt.shape[1]
    return pl.pallas_call(fwd_kernel,
      out_shape=(jax.ShapeDtypeStruct((T,D),BF),jax.ShapeDtypeStruct((D,T),BF),jax.ShapeDtypeStruct((nb,H,L),F32)),
      grid_spec=pltpu.PrefetchScalarGridSpec(num_scalar_prefetch=1,grid=(nb,),
       in_specs=[pl.BlockSpec((D,L),lambda s,a:(0,s)),pl.BlockSpec((n,1,L,256),lambda s,a:(0,s,0,0)),pl.BlockSpec((1,1,L),lambda s,a:(s,0,0))],
       out_specs=(pl.BlockSpec((L,D),lambda s,a:(s,0)),pl.BlockSpec((D,L),lambda s,a:(0,s)),pl.BlockSpec((1,H,L),lambda s,a:(s,0,0))),
       scratch_shapes=[pltpu.VMEM((H,L),F32),pltpu.VMEM((H,L),F32),pltpu.VMEM((D,L),F32),pltpu.VMEM((L,L),F32)]),
      compiler_params=pltpu.CompilerParams(vmem_limit_bytes=40<<20))(lo,qt,kv,starts)
def bwd_kernel(lo_ref, qt_ref, dot_ref, mixt_ref, kv_ref, st_ref, lse_ref, cos_ref, sin_ref, dq_ref, dkv_ref, dl_s, dq_s, bias_s, p_s, ds_s, qs_s, dos_s):
    s=pl.program_id(0); L=qt_ref.shape[1]
    lo=lo_ref[s]; rank=lo_ref[4]
    dkv_ref[...]=jnp.zeros_like(dkv_ref)
    dq_s[...]=jnp.zeros_like(dq_s)
    for h in range(H):
        sl=slice(h*64,(h+1)*64); g,hh=divmod(h,GROUP)
        dl_s[h:h+1,:]=jnp.sum(dot_ref[sl,:].astype(F32)*mixt_ref[sl,:].astype(F32),axis=0,keepdims=True)
        qs_s[g,:,hh*L:(hh+1)*L]=qt_ref[sl,:]
        dos_s[g,:,hh*L:(hh+1)*L]=dot_ref[sl,:]
    def body(kb,_):
        bias_s[...]=bias_of(kb,st_ref,L,rank)
        kvb=kv_ref[kb,0]
        kt=kvb[:,:128].T
        for g in range(2):
            k=kvb[:,g*64:(g+1)*64]
            v=kvb[:,128+g*64:128+(g+1)*64]
            for h in range(g*GROUP,(g+1)*GROUP):
                hh=h-g*GROUP
                sl=slice(h*64,(h+1)*64)
                sc=nn(k,qt_ref[sl,:])+bias_s[...]
                p=jnp.exp(sc-lse_ref[0,h:h+1,:])
                p_s[:,hh*L:(hh+1)*L]=p.astype(BF)
                dp=nn(v,dot_ref[sl,:])
                ds=(p*(dp-dl_s[h:h+1,:])).astype(BF)
                ds_s[:,hh*L:(hh+1)*L]=ds
                dq_s[sl,:]+=nn(kt[g*64:(g+1)*64],ds)
            dk=nt(ds_s[...],qs_s[g])
            dv=nt(p_s[...],dos_s[g])
            dkv_ref[kb,0,:,g*64:(g+1)*64]=dk.astype(BF)
            dkv_ref[kb,0,:,128+g*64:128+(g+1)*64]=dv.astype(BF)
        return 0
    lax.fori_loop(lo,rank+1,body,0)
    c=cos_ref[...]*0.125; sn=sin_ref[...]*0.125
    for h in range(H):
        a=dq_s[h*64:h*64+32,:]; b=dq_s[h*64+32:(h+1)*64,:]
        dq_ref[h*64:h*64+32,:]=(a*c+b*sn).astype(BF)
        dq_ref[h*64+32:(h+1)*64,:]=(b*c-a*sn).astype(BF)
def attn_bwd(lo,qt,dot,mixt,kv,starts,lse,cos,sin):
    n=kv.shape[0]; nb=kv.shape[1]; L=kv.shape[2]; T=qt.shape[1]
    col=lambda r: pl.BlockSpec((r,L),lambda s,a:(0,s))
    return pl.pallas_call(bwd_kernel,
      out_shape=(jax.ShapeDtypeStruct((D,T),BF),jax.ShapeDtypeStruct((n,nb,L,256),BF)),
      grid_spec=pltpu.PrefetchScalarGridSpec(num_scalar_prefetch=1,grid=(nb,),
       in_specs=[col(D),col(D),col(D),pl.BlockSpec((n,1,L,256),lambda s,a:(0,s,0,0)),pl.BlockSpec((1,1,L),lambda s,a:(s,0,0)),pl.BlockSpec((1,H,L),lambda s,a:(s,0,0)),col(32),col(32)],
       out_specs=(col(D),pl.BlockSpec((n,1,L,256),lambda s,a:(0,s,0,0))),
       scratch_shapes=[pltpu.VMEM((H,L),F32),pltpu.VMEM((D,L),F32),pltpu.VMEM((L,L),F32),pltpu.VMEM((L,GROUP*L),BF),pltpu.VMEM((L,GROUP*L),BF),pltpu.VMEM((2,64,GROUP*L),BF),pltpu.VMEM((2,64,GROUP*L),BF)]),
      compiler_params=pltpu.CompilerParams(vmem_limit_bytes=40<<20))(lo,qt,dot,mixt,kv,starts,lse,cos,sin)


def mid_kernel(scale, x_hbm, ct_hbm, mixed_hbm, mixedt_hbm, wout_hbm, gain_ref, wg_ref, wu_ref, wd_ref,
   res_out, gres_out, gmix_out, dwout_out, ggain_out, dw_out,
   c_s, ct_s, n_s, nt_s, resid, acc_o, acc_n, wgu, wdn, hid, ggu, tmp, tmpw, dwbuf, ddbuf, sems, osem, dsem):
    j=pl.program_id(0); nsteps=pl.num_programs(0)
    T=c_s.shape[0]; CH=256 if T%256==0 else T; NCH=T//CH
    slot=lax.rem(j,2)
    def cp(src,dst,k): return pltpu.make_async_copy(src,dst,sems.at[k])
    def gcopies(s,jj):
        out=[]
        for half in range(2):
            for t in range(16):
                out.append(pltpu.make_async_copy(dwbuf.at[s,half,t], dw_out.at[pl.ds(t*76+half*38+2*jj,2)], osem.at[s]))
        out.append(pltpu.make_async_copy(ddbuf.at[s], dw_out.at[pl.ds(1216+32*jj,32)], dsem.at[s]))
        return out
    @pl.when(j==0)
    def _():
        a=cp(ct_hbm,c_s,0); a.start()
        b=cp(mixed_hbm,tmp,1); b.start()
        c=cp(wout_hbm,tmpw,2); c.start()
        d=cp(x_hbm,n_s,3); d.start()
        a.wait();
        for i in range(NCH):
            ct_s[:,i*CH:(i+1)*CH]=c_s[i*CH:(i+1)*CH,:].T
        b.wait(); c.wait(); d.wait()
        for i in range(NCH):
            sl=slice(i*CH,(i+1)*CH)
            r=n_s[sl,:].astype(F32)+nn(tmp[sl,:],tmpw[...])
            resid[sl,:]=r
            inv=lax.rsqrt(jnp.mean(r*r,axis=1,keepdims=True)+norm_eps)
            nv=(r*inv*gain_ref[1:2,:]).astype(BF)
            n_s[sl,:]=nv
            nt_s[:,sl]=nv.T
            acc_o[sl,:]=r
        acc_n[...]=jnp.zeros_like(acc_n)
    @pl.when(j>=2)
    def _():
        for c in gcopies(slot,j-2): c.wait()
    for c in range(2):
        wgu[:,c*128:(c+1)*128]=wg_ref[:,c].reshape(D,128)
        wgu[:,256+c*128:256+(c+1)*128]=wu_ref[:,c].reshape(D,128)
    for c in range(7):
        wdn[:,c*128:(c+1)*128]=wd_ref[:,c].reshape(256,128)
    for i in range(NCH):
        sl=slice(i*CH,(i+1)*CH)
        gu=nn(n_s[sl,:],wgu[...])
        g=gu[:,:256]; u=gu[:,256:]
        gh=nt(c_s[sl,:],wdn[...])
        s=1.0/(1.0+jnp.exp(-g))
        silu=g*s
        h=(silu*u).astype(BF)
        ghs=gh*s
        gg=(ghs*u*(1.0+(g-silu))).astype(BF)
        gu_=(ghs*g).astype(BF)
        hid[sl,:]=h
        ggu[sl,:256]=gg
        ggu[sl,256:]=gu_
        acc_o[sl,:]+=nn(h,wdn[...])
        acc_n[sl,:]+=nt(ggu[sl,:],wgu[...])
    for q in range(0,D,128):
        d=nn(nt_s[q:q+128,:],ggu[...])*scale
        db=d.astype(BF)
        for r in range(16):
            row=q//8+r; t=row//7; w=row%7
            for half in range(2):
                for c in range(2):
                    dwbuf[slot,half,t,c,w]=db[r*8:(r+1)*8,half*256+c*128:half*256+(c+1)*128]
        e=(nn(ct_s[q:q+128,:],hid[...])*scale).astype(BF)
        et=e.T
        ddbuf[slot,:,q//128]=et.reshape(32,8,128)
    for c in gcopies(slot,j): c.start()
    @pl.when(j==nsteps-1)
    def _():
        w=cp(wout_hbm,tmpw,2); w.start()
        b=cp(mixedt_hbm,nt_s,1); b.start()
        w.wait()
        for i in range(NCH):
            sl=slice(i*CH,(i+1)*CH)
            n_s[sl,:]=acc_o[sl,:].astype(BF)
            r=resid[sl,:]; gn=acc_n[sl,:]
            inv=lax.rsqrt(jnp.mean(r*r,axis=1,keepdims=True)+norm_eps)
            ri=r*inv
            gg=jnp.sum(gn*ri,axis=0,keepdims=True)*scale
            if i==0: ggain_out[...]=gg
            else: ggain_out[...]+=gg
            wt=gn*gain_ref[1:2,:]
            m=jnp.mean(r*wt,axis=1,keepdims=True)
            gr=c_s[sl,:].astype(F32)+inv*wt-r*(inv*inv*inv*m)
            acc_n[sl,:]=gr
            gb=gr.astype(BF)
            c_s[sl,:]=gb
            ct_s[:,sl]=nt(tmpw[...],gb).astype(BF)
        o1=cp(n_s,res_out,0); o1.start()
        o2=cp(acc_n,gres_out,3); o2.start()
        o3=cp(ct_s,gmix_out,2); o3.start()
        b.wait()
        for q in range(0,D,128):
            dwout_out[q:q+128,:]=(nn(nt_s[q:q+128,:],c_s[...])*scale).astype(BF)
        o1.wait();o2.wait();o3.wait()
        for c in gcopies(1-slot,j-1): c.wait()
        for c in gcopies(slot,j): c.wait()
def mid(scale,x,ct,mixed,mixedt,wout,gain,wt):
    T=x.shape[0]
    any_=pl.BlockSpec(memory_space=pl.ANY)
    return pl.pallas_call(functools.partial(mid_kernel,scale),
      out_shape=(jax.ShapeDtypeStruct((T,D),BF),jax.ShapeDtypeStruct((T,D),F32),jax.ShapeDtypeStruct((D,T),BF),
        jax.ShapeDtypeStruct((D,D),BF),jax.ShapeDtypeStruct((1,D),F32),jax.ShapeDtypeStruct((1824,7,8,128),BF)),
      grid=(STEPS,),
      in_specs=[any_,any_,any_,any_,any_,pl.BlockSpec((2,D),lambda j:(0,0)),
        pl.BlockSpec((16,2,7,8,128),lambda j:(0,j,0,0,0)),
        pl.BlockSpec((16,2,7,8,128),lambda j:(0,STEPS+j,0,0,0)),
        pl.BlockSpec((32,7,8,128),lambda j:(38+j,0,0,0))],
      out_specs=(any_,any_,any_,pl.BlockSpec((D,D),lambda j:(0,0)),pl.BlockSpec((1,D),lambda j:(0,0)),any_),
      scratch_shapes=[pltpu.VMEM((T,D),BF),pltpu.VMEM((D,T),BF),pltpu.VMEM((T,D),BF),pltpu.VMEM((D,T),BF),
        pltpu.VMEM((T,D),F32),pltpu.VMEM((T,D),F32),pltpu.VMEM((T,D),F32),
        pltpu.VMEM((D,512),BF),pltpu.VMEM((256,D),BF),pltpu.VMEM((T,256),BF),pltpu.VMEM((T,512),BF),
        pltpu.VMEM((T,D),BF),pltpu.VMEM((D,D),BF),
        pltpu.VMEM((2,2,16,2,7,8,128),BF),pltpu.VMEM((2,32,7,8,128),BF),
        pltpu.SemaphoreType.DMA((4,)),pltpu.SemaphoreType.DMA((2,)),pltpu.SemaphoreType.DMA((2,))],
      compiler_params=pltpu.CompilerParams(vmem_limit_bytes=60<<20))(x,ct,mixed,mixedt,wout,gain,wt.reshape(24,76,7,8,128),wt.reshape(24,76,7,8,128),wt.reshape(1824,7,8,128))


def per_device(
    inputs,
    cotangent,
    segments,
    positions,
    attn_master,
    attn_moment,
    attn_second,
    ffn_master,
    ffn_moment,
    ffn_second,
):
    count, span = inputs.shape[0], inputs.shape[1]
    parts = lax.axis_size("seq")
    rank = lax.axis_index("seq")
    tokens = count * span
    scale = 1.0 / math.sqrt(tokens * parts * lax.axis_size("dp"))
    aligned = ffn_master.shape[0] % (PIECE * 128) == 0
    attn_flat = lax.all_gather(attn_master.reshape(-1, 128).astype(BF), "seq", axis=0, tiled=True)
    seg_all = lax.all_gather(segments, "seq", axis=0, tiled=False)
    if aligned:
        pieces = ffn_master.shape[0] // (PIECE * 128)
        kinds = (rank * pieces + jnp.arange(pieces, dtype=jnp.int32) >= GU_PIECES).astype(jnp.int32)
        mine = pack(kinds, ffn_master.reshape(-1, 128))
        tiles = lax.all_gather(mine, "seq", axis=0, tiled=True)
    else:
        tiles = tiles_of_flat(lax.all_gather(ffn_master.astype(BF), "seq", axis=0, tiled=True))
    x = inputs.reshape(tokens, D)
    frequency = jnp.exp(jnp.arange(HD // 2, dtype=F32) * (-2.0 * math.log(rope_base) / HD))
    angles = frequency[:, None] * positions.reshape(1, tokens).astype(F32)
    cos, sin = jnp.cos(angles), jnp.sin(angles)
    qt, kv, normed_t, wqkv, wout, gains = qkv_forward(x, attn_flat, cos, sin, count)
    kv_all = lax.all_gather(kv, "seq", axis=0, tiled=False)
    starts = jnp.sum(
        (seg_all.transpose(1, 0, 2).reshape(count, 1, parts * span) < segments[:, :, None]).astype(jnp.int32),
        axis=2,
    )
    bounds = jnp.concatenate([starts[:, 0] // span, rank[None].astype(jnp.int32)])
    starts = starts[:, None, :]
    mixed, mixed_t, log_total = attn_fwd(bounds, qt, kv_all, starts)
    result, grad_res, grad_mixed_t, dwout, ggain, dtiles = mid(
        scale, x, cotangent.reshape(tokens, D), mixed, mixed_t, wout, gains, tiles
    )
    dtiles = dtiles.reshape(tiles.shape)
    if aligned:
        owned = lax.psum_scatter(dtiles, "seq", scatter_dimension=0, tiled=True)
    else:
        owned = lax.psum_scatter(flat_of_tiles(dtiles), "seq", scatter_dimension=0, tiled=True)
    owned = lax.psum(owned, "dp")
    dq, dkv = attn_bwd(bounds, qt, grad_mixed_t, mixed_t, kv_all, starts, log_total, cos, sin)
    dkv = lax.psum_scatter(dkv, "seq", scatter_dimension=0, tiled=False)
    grad_input, dattn = tail_backward(
        scale, attn_flat.shape[0], dq, dkv, x, normed_t, wqkv, gains, cos, sin, grad_res, dwout, ggain
    )
    grad_attn = lax.psum_scatter(dattn, "seq", scatter_dimension=0, tiled=True)
    grad_attn, owned = lax.optimization_barrier((grad_attn, owned))
    grad_attn = lax.psum(grad_attn, "dp").astype(F32).reshape(attn_master.shape)
    attn_change, moment_attn, second_attn = adam_step(
        attn_master, attn_moment, attn_second, grad_attn
    )
    if aligned:
        ffn_change, moment_ffn, second_ffn, grad_ffn = (
            v.reshape(ffn_master.shape)
            for v in adam_tiles(
                kinds, owned, *(v.reshape(-1, 128) for v in (ffn_master, ffn_moment, ffn_second))
            )
        )
    else:
        grad_ffn = owned.astype(F32)
        ffn_change, moment_ffn, second_ffn = adam_step(ffn_master, ffn_moment, ffn_second, grad_ffn)
    return (
        result.reshape(inputs.shape),
        grad_input.reshape(inputs.shape),
        attn_change,
        moment_attn,
        second_attn,
        grad_attn,
        ffn_change,
        moment_ffn,
        second_ffn,
        grad_ffn,
    )


def solution(mesh):
    rows, flat = P("dp", "seq", None), P("seq")
    return jax.shard_map(
        per_device,
        mesh=mesh,
        in_specs=(rows, rows, P("dp", "seq"), P("dp", "seq")) + (flat,) * 6,
        out_specs=(rows, rows) + (flat,) * 8,
        check_vma=False,
    )
```

time: 1700 us -> 763 us (0.45)
  matrix products: 548 us -> 0 us
  other arithmetic: 304 us -> 8.16 us
  local copies, waits for them, and re-layouts: 271 us -> 25.2 us
  Pallas kernels: 0 us -> 213 us
  waiting for transfers between devices: 538 us -> 440 us
  blocking collectives: 8.86 us -> 51.3 us
    dot_general x36 -> x0, matrix products: 548 us -> none  [the longest x3 98.9 us: delta_pass(): jnp.einsum('sckgd,sbkd->skgcb', grad_mixed, value_block, preferred_elemen...]
    unnamed x9 -> x8, waiting for transfers between devices: 356 us -> 0.12 us
    pallas_call x0 -> x7, Pallas kernels: none -> 213 us  [the longest x1 127 us: mid(): pl.pallas_call(functools.partial(mid_kernel, scale), out_shape=(jax.Shape...]
    reduce_scatter x2, waiting for transfers between devices: 0.04 us -> 189 us  [the longest x1 134 us: per_device(): owned = lax.psum_scatter(dtiles, 'seq', scatter_dimension=0, tiled=True)]
    convert_element_type x10 -> x1, other arithmetic: 132 us -> 0.01 us  [per_device(): (rank * pieces + jnp.arange(pieces, dtype=jnp.int32) >= GU_PIECES).astype...]
    all_gather x4 -> x3, waiting for transfers between devices: 61.1 us -> 167 us  [the longest x1 110 us: per_device(): tiles = lax.all_gather(mine, 'seq', axis=0, tiled=True)]
    slice x17 -> x1, local copies, waits for them, and re-layouts: 96.8 us -> 0.12 us  [per_device(): starts[:, 0] // span]
    all_gather x1 -> x0, other arithmetic: 79.1 us -> none  [per_device(): lax.all_gather(attn_master.astype(jnp.bfloat16), 'seq', axis=0, tiled=True)]
  transfers between devices with their start and end apart: 8 -> 8, of which waited for: 4 -> 7; matrix products, arithmetic and copies ran while one was open for 23% -> 6% of each run, Pallas kernels for 0% -> 10%
where the time goes in v1:
time: 763 us; the launch traced here: 754 us
  waiting for transfers between devices  440 us (58%)
  Pallas kernels  213 us (28%)
  blocking collectives  51.3 us (7%)
  local copies, waits for them, and re-layouts  25.2 us (3%)
  between operations  15.1 us (2%)
  other arithmetic  8.16 us (1%)
    reduce_scatter x1, waiting for transfers between devices, per_device(): owned = lax.psum_scatter(dtiles, 'seq', scatter_dimension=0, tiled=True)  134 us
    pallas_call x1, Pallas kernels, mid(): pl.pallas_call(functools.partial(mid_kernel, scale), out_shape=(jax.Shape...  127 us
    all_gather x1, waiting for transfers between devices, per_device(): tiles = lax.all_gather(mine, 'seq', axis=0, tiled=True)  110 us
    psum x1, waiting for transfers between devices, per_device(): owned = lax.psum(owned, 'dp')  66 us
    reduce_scatter x1, waiting for transfers between devices, per_device(): dkv = lax.psum_scatter(dkv, 'seq', scatter_dimension=0, tiled=False)  55.1 us
    unnamed x1, blocking collectives  42.1 us
    all_gather x1, waiting for transfers between devices, per_device(): lax.all_gather(attn_master.reshape(-1, 128).astype(BF), 'seq', axis=0, ti...  36.5 us
    unnamed x39, local copies, waits for them, and re-layouts  24.1 us
  transfers between devices with their start and end apart: 8, of which 7 were waited for; matrix products, arithmetic and copies ran while one was open for 6% of the time, Pallas kernels for 10%

profile of v1, /device:TPU:0, one launch (start us, length us, event | category | flops | bytes accessed | tf_op | source)
XLA Modules:
  0.0 754.3 jit_solution(4546065215709443372)
XLA Ops:
  7.2 0.0 all-gather.12.cloned.1.call-start
  7.2 2.0 convert_bitcast_fusion
  9.2 0.0 all-gather.10.cloned.1.call-start
  9.3 0.7 convert_bitcast_fusion.1
  10.0 1.2 multiply_sine_fusion
  11.2 36.5 %all-gather.12.cloned.1.call-done = bf16[8,1795,128]{2,1,0:T(8,128)(2,1)} async-done(((bf16[1,1795,128]{2,1,0:T(8,128)(2,1)}), bf16[8,1795,128]{2,1,0:T(8,128)(2,1)}) %all-gather.12.cloned.1.call-update) | async-done | bytes 3676176 | tf_op jit(solution)/shard_map/all_gather | solution.py:557
  47.8 5.0 reshape.110.flat_ref
  52.7 10.2 %qkv_forward.1 = (bf16[896,1024]{1,0:T(8,128)(2,1)}, bf16[4,256,256]{2,1,0:T(8,128)(2,1)}, bf16[896,1024]{1,0:T(8,128)(2,1)}, bf16[896,1152]{1,0:T(8,128)(2,1)},...) custom-call(bf16[1024,896]{1,0:T(8,128)(2,1)} %bitcast.38, bf16[14360,128]{1,0:T(8,128)(2,1)} %reshape.110.flat_ref, ...), custom_call_target="tpu_custom_call" | custom-call | tf_op jit(solution)/shard_map/qkv_forward/pallas_call | solution.py:225
  63.0 0.0 all-gather.10.cloned.1.call-update
  63.0 0.0 all-gather.8.cloned.1.call-start
  63.1 2.8 copy-done
  65.9 3.1 pack_ffn.1
  69.0 0.0 reduce-scatter.7.cloned.1.call-start
  69.1 9.2 %all-gather.2 = s32[8,4,256]{2,1,0:T(4,128)S(1)} all-gather(s32[1,4,256]{2,1,0:T(4,128)S(1)} %bitcast.48), channel_id=2, replica_groups=mesh['dp'=4,'seq'=8] {'seq'}, dimensions={0}, use_global_device_ids=true | all-gather | bytes 36864 | tf_op jit(solution)/shard_map/all_gather | solution.py:558
  78.3 1.1 convert_reduce_fusion
  79.4 0.1 slice_reduce_fusion
  79.5 0.1 pad_add_fusion.lo_ref
  79.6 20.4 %all-gather.10.cloned.1.call-done = bf16[32,256,256]{2,1,0:T(8,128)(2,1)} async-done(((bf16[4,256,256]{2,1,0:T(8,128)(2,1)}), bf16[32,256,256]{2,1,0:T(8,128)(2,1)}) %all-gather.10.cloned.1.call-update) | async-done | bytes 4194320 | tf_op jit(solution)/shard_map/all_gather | solution.py:571
  100.0 2.2 copy-done.1
  102.1 17.3 %shard_map.177 = (bf16[1024,896]{1,0:T(8,128)(2,1)S(1)}, bf16[896,1024]{1,0:T(8,128)(2,1)S(1)}, f32[4,14,256]{2,1,0:T(8,128)S(1)}) custom-call(s32[5]{0:T(128)S(1)} %pad_add_fusion.lo_ref, bf16[896,1024]{1,0:T(8,128)(2,1)S(1)} %copy-done.2, bf16[8,4,256,256]{3,2,1,0:T(8,128)(2,1)S(1)} %bitcast.33, s32[4,1,256]{2,1,0:T(1,128)S(1)} %broadcast_in_dim.9.st_ref), custom_call_target="tpu_custom_call" | custom-call | tf_op jit(solution)/shard_map/pallas_call | solution.py:361
  119.4 1.2 copy-done.3
  120.7 1.2 copy-done.11
  121.9 110.1 %all-gather.8.cloned.1.call-done = bf16[12768,8,128]{2,1,0:T(8,128)(2,1)} async-done(((bf16[1596,8,128]{2,1,0:T(8,128)(2,1)}), bf16[12768,8,128]{2,1,0:T(8,128)(2,1)}) %all-gather.8.cloned.1.call-update) | async-done | bytes 26148880 | tf_op jit(solution)/shard_map/all_gather | solution.py:563
  232.0 127.2 %shard_map.178 = (bf16[1024,896]{1,0:T(8,128)(2,1)}, f32[1024,896]{1,0:T(8,128)}, bf16[896,1024]{1,0:T(8,128)(2,1)}, bf16[896,896]{1,0:T(8,128)(2,1)}, f32[1,896...) custom-call(bf16[1024,896]{1,0:T(8,128)(2,1)} %bitcast.39, bf16[1024,896]{1,0:T(8,128)(2,1)} %bitcast.44, ...), custom_call_target="tpu_custom_call" | custom-call | tf_op jit(solution)/shard_map/pallas_call | solution.py:521
  359.2 0.0 reduce-scatter.7.cloned.1.call-update
  359.3 0.0 reduce-scatter.5.cloned.1.call-start
  359.3 0.8 copy-done.7
  360.1 0.1 copy-done.8
  360.2 1.5 copy-done.4
  361.7 1.5 copy-done.10
  363.2 20.8 %shard_map.179 = (bf16[896,1024]{1,0:T(8,128)(2,1)S(1)}, bf16[8,4,256,256]{3,2,1,0:T(8,128)(2,1)S(1)}) custom-call(s32[5]{0:T(128)S(1)} %pad_add_fusion.lo_ref, bf16[896,1024]{1,0:T(8,128)(2,1)S(1)} %copy-done.2, bf16[896,1024]{1,0:T(8,128)(2,1)S(1)} %copy-done.10, bf16[896,1024]{1,0:T(8,128)(2,1)S(1)} %copy-done.4, bf16[8,4,256,256]{3,2,1,0:T(8,128)(2,1)} %bitcast.32, ...), custom_call_target="tpu_custom_call" | custom-call | tf_op jit(solution)/shard_map/pallas_call | solution.py:409
  384.0 2.5 copy-done.5
  386.6 1.2 copy-done.9
  387.8 0.0 all-reduce.5.cloned.1.call-start
  387.9 134.3 %reduce-scatter.7.cloned.1.call-done = bf16[1596,8,128]{2,1,0:T(8,128)(2,1)} async-done(((bf16[12768,8,128]{2,1,0:T(8,128)(2,1)}), bf16[1596,8,128]{2,1,0:T(8,128)(2,1)}) %reduce-scatter.7.cloned.1.call-update) | async-done | bytes 3268624 | tf_op jit(solution)/shard_map/reduce_scatter | solution.py:584
  522.2 0.0 all-reduce.7.cloned.1.call-start
  522.2 55.1 %reduce-scatter.5.cloned.1.call-done = bf16[1,4,256,256]{3,2,1,0:T(8,128)(2,1)} async-done(((bf16[8,4,256,256]{3,2,1,0:T(8,128)(2,1)}), bf16[1,4,256,256]{3,2,1,0:T(8,128)(2,1)}) %reduce-scatter.5.cloned.1.call-update) | async-done | bytes 524304 | tf_op jit(solution)/shard_map/reduce_scatter | solution.py:589
  577.3 14.4 %tail_backward.1 = (f32[1024,896]{1,0:T(8,128)}, bf16[14360,128]{1,0:T(8,128)(2,1)}) custom-call(bf16[896,1024]{1,0:T(8,128)(2,1)} %copy-done.9, bf16[4,256,256]{2,1,0:T(8,128)(2,1)} %bitcast.45, bf16[1024,896]{1,0:T(8,128)(2,1)} %bitcast.40, bf16[896,1024]{1,0:T(8,128)(2,1)} %get-tuple-element.46.nt_ref, bf16[896,1152]{1,0:T(8,128)(2,1)} %get-tuple-element.47.wqkv_ref, ...), custom_call_target="tpu_custom_call" | custom-call | tf_op jit(solution)/shard_map/tail_backward/pallas_call | solution.py:311
  591.7 42.1 %fusion = bf16[1808,128]{1,0:T(8,128)(2,1)S(1)} fusion(bf16[14360,128]{1,0:T(8,128)(2,1)} %get-tuple-element.52), kind=kCustom, calls=%all-reduce-scatter | all-reduce-scatter fusion | flops 1851393 | bytes 4139520
  633.9 1.3 collective-permute-start
  635.2 0.6 dynamic-slice.4
  636.4 1.5 concatenate.4
  637.9 0.9 constant_dynamic-slice_fusion
  638.8 66.0 %all-reduce.5.cloned.1.call-done.g_ref = bf16[1596,8,128]{2,1,0:T(8,128)(2,1)} async-done(((bf16[1596,8,128]{2,1,0:T(8,128)(2,1)}), bf16[1596,8,128]{2,1,0:T(8,128)(2,1)}) %all-reduce.5.cloned.1.call-update) | async-done | bytes 3268624 | tf_op jit(solution)/shard_map/psum | solution.py:587
  704.8 1.9 copy-done.6
  706.8 20.4 %adam_ffn.1 = (f32[12768,128]{1,0:T(8,128)}, f32[12768,128]{1,0:T(8,128)}, f32[12768,128]{1,0:T(8,128)}, f32[12768,128]{1,0:T(8,128)}) custom-call(s32[3]{0:T(128)S(1)} %compare_convert_fusion.kind_ref, bf16[1596,8,128]{2,1,0:T(8,128)(2,1)S(1)} %copy-done.6, f32[12768,128]{1,0:T(8,128)} %bitcast.30, f32[12768,128]{1,0:T(8,128)} %bitcast.41, ...), custom_call_target="tpu_custom_call" | custom-call | tf_op jit(solution)/shard_map/adam_ffn/pallas_call | solution.py:138
  727.2 17.0 %all-reduce.7.cloned.1.call-done = bf16[229760]{0:T(1024)(128)(2,1)} async-done(((bf16[229760]{0:T(1024)(128)(2,1)}), bf16[229760]{0:T(1024)(128)(2,1)}) %all-reduce.7.cloned.1.call-update) | async-done | bytes 459536 | tf_op jit(solution)/shard_map/psum | solution.py:595
  744.3 3.0 add_multiply_fusion
  (35 shorter events, 0.2 us)
Async XLA Ops:
  7.2 40.6 %all-gather.12.cloned.1.call-start = ((), (), s32[]{:S(2)}) async-start(), calls=%async_computation.8 | async-start | bytes 4147200 | tf_op jit(solution)/shard_map/all_gather | solution.py:557
  9.2 90.7 %all-gather.10.cloned.1.call-start = ((), (), s32[]{:S(2)}) async-start(), calls=%async_computation.7 | async-start | bytes 4718592 | tf_op jit(solution)/shard_map/all_gather | solution.py:571
  63.0 169.0 %all-gather.8.cloned.1.call-start = ((), (), s32[]{:S(2)}) async-start(), calls=%async_computation.2 | async-start | bytes 29417472 | tf_op jit(solution)/shard_map/all_gather | solution.py:563
  63.1 2.9 copy-start
  65.9 3.2 copy-start.15
  69.0 30.9 %copy-start.2 = (bf16[896,1024]{1,0:T(8,128)(2,1)S(1)}, bf16[896,1024]{1,0:T(8,128)(2,1)}, u32[]{:S(2)}) copy-start(bf16[896,1024]{1,0:T(8,128)(2,1)} %get-tuple-element.35.qt_ref) | copy-start | bytes 5505028
  69.0 453.1 %reduce-scatter.7.cloned.1.call-start = ((), (), s32[]{:S(2)}) async-start(), calls=%async_computation.4 | async-start | bytes 29417472 | tf_op jit(solution)/shard_map/reduce_scatter | solution.py:584
  100.0 2.2 copy-start.1
  119.4 1.2 copy-start.3
  120.7 1.2 copy-start.11
  359.2 0.9 copy-start.7
  359.2 1.0 copy-start.8
  359.3 218.0 %reduce-scatter.5.cloned.1.call-start = ((), (), s32[]{:S(2)}) async-start(), calls=%async_computation.3 | async-start | bytes 4718592 | tf_op jit(solution)/shard_map/reduce_scatter | solution.py:589
  360.2 1.5 copy-start.4
  361.7 1.5 copy-start.10
  384.0 2.6 copy-start.5
  386.6 1.2 copy-start.9
  387.8 317.0 %all-reduce.5.cloned.1.call-start = ((), (), s32[]{:S(2)}) async-start(), calls=%async_computation.5 | async-start | bytes 6537216 | tf_op jit(solution)/shard_map/psum | solution.py:587
  522.2 222.1 %all-reduce.7.cloned.1.call-start = ((), (), s32[]{:S(2)}) async-start(), calls=%async_computation.6 | async-start | bytes 921600 | tf_op jit(solution)/shard_map/psum | solution.py:595
  591.7 43.5 %copy-start.16 = (u32[32]{0:T(128)S(1)}, u32[32]{0:T(128)}, u32[]{:S(2)}) copy-start(u32[32]{0:T(128)} %constant.47) | copy-start | bytes 388
  633.9 2.6 collective-permute-start
  704.8 1.9 copy-start.6
  706.7 37.5 %copy-start.12 = (f32[229760]{0:T(1024)S(1)}, f32[229760]{0:T(1024)}, u32[]{:S(2)}) copy-start(f32[229760]{0:T(1024)} %param.14) | copy-start | bytes 2757124
  706.8 37.5 %copy-start.13 = (f32[229760]{0:T(1024)S(1)}, f32[229760]{0:T(1024)}, u32[]{:S(2)}) copy-start(f32[229760]{0:T(1024)} %param.15) | copy-start | bytes 2757124
  706.8 37.5 %copy-start.14 = (f32[229760]{0:T(1024)S(1)}, f32[229760]{0:T(1024)}, u32[]{:S(2)}) copy-start(f32[229760]{0:T(1024)} %param.16) | copy-start | bytes 2757124
Sparse Core Ops, SparseCore 0:
  10.5 37.2 all-gather.11
  63.1 36.7 all-gather.9
  102.4 129.5 all-gather.7
  359.4 162.6 reduce-scatter.6
  525.9 51.3 reduce-scatter.4
  579.6 125.1 all-reduce.4
  707.9 36.3 all-reduce.6
